TPU v7x, 32 devices: a whole 2x2x4 slice. The times are simulated.
32 devices in a mesh: dp: 8 (over z, y), seq: 4 (over x, core).
Axes of the slice: x: 2, y: 2, z: 4, core: 2. Of those that a mesh axis runs over, the one named last changes fastest.
Arguments:
- tokens: bfloat16 [8, 1024, 1024], P('dp', 'seq'), may hold values from -6 to 6
- lead_hours: int32 [8], P('dp'), may hold values from 6 to 168
- valid_counts: int32 [8], P('dp'), may hold values from 769 to 1024
- patch_mask: int32 [8, 1024], P('dp', 'seq'), may hold values 0 or 1
- first_gain: bfloat16 [1024], P(('dp', 'seq')), may hold values from 0.099609375 to 1.8984375
- first_shift: bfloat16 [1024], P(('dp', 'seq')), may hold values from -4 to 4
- qkv_weight: bfloat16 [1024, 3072], P(('dp', 'seq')), may hold values from -0.1875 to 0.1875
- query_bias: bfloat16 [1024], P(('dp', 'seq')), may hold values from -6 to 6
- value_bias: bfloat16 [1024], P(('dp', 'seq')), may hold values from -0.3125 to 0.3125
- out_weight: bfloat16 [1024, 1024], P(('dp', 'seq')), may hold values from -4 to 4
- out_bias: bfloat16 [1024], P(('dp', 'seq')), may hold values from -4 to 4
- second_gain: bfloat16 [1024], P(('dp', 'seq')), may hold values from 0.099609375 to 1.8984375
- second_shift: bfloat16 [1024], P(('dp', 'seq')), may hold values from -4 to 4
- up_weight: bfloat16 [1024, 4096], P(('dp', 'seq')), may hold values from -0.1875 to 0.1875
- up_bias: bfloat16 [4096], P(('dp', 'seq')), may hold values from -6 to 6
- down_weight: bfloat16 [4096, 1024], P(('dp', 'seq')), may hold values from -0.09375 to 0.09375
- down_bias: bfloat16 [1024], P(('dp', 'seq')), may hold values from -4 to 4
- lead_weight: bfloat16 [1024], P(('dp', 'seq')), may hold values from -6 to 6
- lead_bias: bfloat16 [1024], P(('dp', 'seq')), may hold values from -4 to 4
- cotangent: bfloat16 [8, 1024, 1024], P('dp', 'seq'), may hold values from -6 to 6
Outputs:
- block_out: bfloat16 [8, 1024, 1024], P('dp', 'seq')
- tokens_grad: bfloat16 [8, 1024, 1024], P('dp', 'seq')
- first_gain_grad: float32 [1024], P(('dp', 'seq'))
- first_shift_grad: float32 [1024], P(('dp', 'seq'))
- qkv_weight_grad: float32 [1024, 3072], P(('dp', 'seq'))
- query_bias_grad: float32 [1024], P(('dp', 'seq'))
- value_bias_grad: float32 [1024], P(('dp', 'seq'))
- out_weight_grad: float32 [1024, 1024], P(('dp', 'seq'))
- out_bias_grad: float32 [1024], P(('dp', 'seq'))
- second_gain_grad: float32 [1024], P(('dp', 'seq'))
- second_shift_grad: float32 [1024], P(('dp', 'seq'))
- up_weight_grad: float32 [1024, 4096], P(('dp', 'seq'))
- up_bias_grad: float32 [4096], P(('dp', 'seq'))
- down_weight_grad: float32 [4096, 1024], P(('dp', 'seq'))
- down_bias_grad: float32 [1024], P(('dp', 'seq'))
- lead_weight_grad: float32 [1024], P(('dp', 'seq'))
- lead_bias_grad: float32 [1024], P(('dp', 'seq'))
All inputs are finite; a program needn't handle non-finite values. No bound on the sum of `patch_mask` on one device may be relied on, other than what follows from the above.
Results may differ from a plain program's by a relative error of at most 0.014.
Values may be sent and summed in bfloat16 or wider, within the bound.
No kernel may reach another device: no remote copies, remote signals or barrier semaphores. Data moves between devices by JAX's collectives and lax.ppermute only.
A program may use at most 256 MiB of HBM per device.

v0:
```python
import math

import jax
import jax.numpy as jnp
from jax import lax
from jax.sharding import PartitionSpec as P

HEADS = 16
HEAD_DIM = 64


EPSILON = 1e-06
MASKED = -1e30


def layer_norm(values, norm_gain, offset):
    row_mean = jnp.mean(values, axis=-1, keepdims=True)
    centered = values - row_mean
    spread = jnp.mean(centered * centered, axis=-1, keepdims=True)
    return centered * lax.rsqrt(spread + EPSILON) * norm_gain + offset


def collect_weights(shards):
    (
        first_gain,
        first_shift,
        qkv_weight,
        query_bias,
        value_bias,
        out_weight,
        out_bias,
        second_gain,
        second_shift,
        up_weight,
        up_bias,
        down_weight,
        down_bias,
        lead_weight,
        lead_bias,
    ) = shards
    gathered = (
        lax.all_gather(first_gain, ("dp", "seq"), axis=0, tiled=True),
        lax.all_gather(first_shift, ("dp", "seq"), axis=0, tiled=True),
        lax.all_gather(qkv_weight, ("dp", "seq"), axis=0, tiled=True),
        lax.all_gather(query_bias, ("dp", "seq"), axis=0, tiled=True),
        lax.all_gather(value_bias, ("dp", "seq"), axis=0, tiled=True),
        lax.all_gather(out_weight, ("dp", "seq"), axis=0, tiled=True),
        lax.all_gather(out_bias, ("dp", "seq"), axis=0, tiled=True),
        lax.all_gather(second_gain, ("dp", "seq"), axis=0, tiled=True),
        lax.all_gather(second_shift, ("dp", "seq"), axis=0, tiled=True),
        lax.all_gather(up_weight, ("dp", "seq"), axis=0, tiled=True),
        lax.all_gather(up_bias, ("dp", "seq"), axis=0, tiled=True),
        lax.all_gather(down_weight, ("dp", "seq"), axis=0, tiled=True),
        lax.all_gather(down_bias, ("dp", "seq"), axis=0, tiled=True),
        lax.all_gather(lead_weight, ("dp", "seq"), axis=0, tiled=True),
        lax.all_gather(lead_bias, ("dp", "seq"), axis=0, tiled=True),
    )
    return gathered


def group_probs(head_queries, head_keys, key_valid, score_scale):
    scores = (
        jnp.einsum("qgd,kgd->gqk", head_queries, head_keys, preferred_element_type=jnp.float32)
        * score_scale
    )
    scores = jnp.where(key_valid[None, None, :], scores, MASKED)
    top_score = jnp.max(scores, axis=-1, keepdims=True)
    expo_scores = jnp.exp(scores - top_score)
    return expo_scores / jnp.sum(expo_scores, axis=-1, keepdims=True)


def forward_pass(tokens, lead_scaled, key_valid, weights):
    (
        first_gain,
        first_shift,
        qkv_weight,
        query_bias,
        value_bias,
        out_weight,
        out_bias,
        second_gain,
        second_shift,
        up_weight,
        up_bias,
        down_weight,
        down_bias,
        lead_weight,
        lead_bias,
    ) = weights
    model_width = tokens.shape[-1]
    start_sum = (
        tokens[0].astype(jnp.float32)
        + lead_scaled * lead_weight.astype(jnp.float32)
        + lead_bias.astype(jnp.float32)
    )
    normed = layer_norm(
        start_sum, first_gain.astype(jnp.float32), first_shift.astype(jnp.float32)
    ).astype(jnp.bfloat16)
    projected = jnp.dot(normed, qkv_weight, preferred_element_type=jnp.float32)
    queries = (projected[:, :model_width] + query_bias.astype(jnp.float32)).astype(jnp.bfloat16)
    key_rows = projected[:, model_width : 2 * model_width].astype(jnp.bfloat16)
    value_rows = (projected[:, 2 * model_width :] + value_bias.astype(jnp.float32)).astype(
        jnp.bfloat16
    )
    all_keys, all_values = (
        lax.all_gather(key_rows, "seq", axis=0, tiled=True),
        lax.all_gather(value_rows, "seq", axis=0, tiled=True),
    )
    score_scale = 1.0 / math.sqrt(HEAD_DIM)
    row_count = queries.shape[0]
    key_count = all_keys.shape[0]
    split_queries = queries.reshape(row_count, HEADS, HEAD_DIM)
    split_keys = all_keys.reshape(key_count, HEADS, HEAD_DIM)
    split_values = all_values.reshape(key_count, HEADS, HEAD_DIM)
    pieces = []
    for first_head in range(0, HEADS, 4):
        head_probs = group_probs(
            split_queries[:, first_head : first_head + 4],
            split_keys[:, first_head : first_head + 4],
            key_valid,
            score_scale,
        )
        low_probs = head_probs.astype(jnp.bfloat16)
        head_out = jnp.einsum(
            "gqk,kgd->qgd",
            low_probs,
            split_values[:, first_head : first_head + 4],
            preferred_element_type=jnp.float32,
        )
        pieces.append(head_out.reshape(row_count, 4 * HEAD_DIM))
    attended = jnp.concatenate(pieces, axis=1).astype(jnp.bfloat16)
    middle = start_sum + (
        jnp.dot(attended, out_weight, preferred_element_type=jnp.float32)
        + out_bias.astype(jnp.float32)
    )
    normed_two = layer_norm(
        middle, second_gain.astype(jnp.float32), second_shift.astype(jnp.float32)
    ).astype(jnp.bfloat16)
    hidden_pre = jnp.dot(
        normed_two, up_weight, preferred_element_type=jnp.float32
    ) + up_bias.astype(jnp.float32)
    hidden = jax.nn.gelu(hidden_pre, approximate=False).astype(jnp.bfloat16)
    block_out = (
        middle
        + (
            jnp.dot(hidden, down_weight, preferred_element_type=jnp.float32)
            + down_bias.astype(jnp.float32)
        )
    ).astype(jnp.bfloat16)
    return (
        start_sum,
        normed,
        split_queries,
        split_keys,
        split_values,
        attended,
        middle,
        normed_two,
        hidden_pre,
        hidden,
        block_out,
    )


def gelu_exact(values):
    return jax.nn.gelu(values, approximate=False)


def body(
    tokens,
    lead_hours,
    valid_counts,
    patch_mask,
    first_gain,
    first_shift,
    qkv_weight,
    query_bias,
    value_bias,
    out_weight,
    out_bias,
    second_gain,
    second_shift,
    up_weight,
    up_bias,
    down_weight,
    down_bias,
    lead_weight,
    lead_bias,
    cotangent,
):
    shards = (
        first_gain,
        first_shift,
        qkv_weight,
        query_bias,
        value_bias,
        out_weight,
        out_bias,
        second_gain,
        second_shift,
        up_weight,
        up_bias,
        down_weight,
        down_bias,
        lead_weight,
        lead_bias,
    )
    row_count = tokens.shape[1]
    model_width = tokens.shape[2]
    key_count = row_count * lax.axis_size("seq")
    lead_scaled = lead_hours[0].astype(jnp.float32) / 100.0
    key_valid = jnp.arange(key_count, dtype=jnp.int32) < valid_counts[0]
    positions = lax.axis_index("seq") * row_count + jnp.arange(row_count, dtype=jnp.int32)
    loss_weight = (patch_mask[0] * (positions < valid_counts[0]).astype(jnp.int32)).astype(
        jnp.float32
    )
    weights = collect_weights(shards)
    saved = forward_pass(tokens, lead_scaled, key_valid, weights)
    block_out = saved[10]
    back_weights = collect_weights(shards)
    back_saved = forward_pass(tokens, lead_scaled, key_valid, back_weights)
    (
        full_gain_one,
        full_shift_one,
        full_qkv,
        full_query_bias,
        full_value_bias,
        full_out,
        full_out_bias,
        full_gain_two,
        full_shift_two,
        full_up,
        full_up_bias,
        full_down,
        full_down_bias,
        full_lead_weight,
        full_lead_bias,
    ) = back_weights
    (
        start_sum,
        normed,
        split_queries,
        split_keys,
        split_values,
        attended,
        middle,
        normed_two,
        hidden_pre,
        hidden,
        unused_out,
    ) = back_saved
    grad_out = (cotangent[0].astype(jnp.float32) * loss_weight[:, None]).astype(jnp.bfloat16)
    down_weight_grad = jnp.einsum("rf,rd->fd", hidden, grad_out, preferred_element_type=jnp.float32)
    down_bias_grad = jnp.sum(grad_out.astype(jnp.float32), axis=0)
    grad_hidden = jnp.einsum("rd,fd->rf", grad_out, full_down, preferred_element_type=jnp.float32)
    gelu_value, gelu_back = jax.vjp(gelu_exact, hidden_pre)
    grad_pre = gelu_back(grad_hidden)[0].astype(jnp.bfloat16)
    up_weight_grad = jnp.einsum(
        "rd,rf->df", normed_two, grad_pre, preferred_element_type=jnp.float32
    )
    up_bias_grad = jnp.sum(grad_pre.astype(jnp.float32), axis=0)
    grad_normed_two = jnp.einsum("rf,df->rd", grad_pre, full_up, preferred_element_type=jnp.float32)
    norm_value, second_back = jax.vjp(
        layer_norm, middle, full_gain_two.astype(jnp.float32), full_shift_two.astype(jnp.float32)
    )
    middle_part, second_gain_grad, second_shift_grad = second_back(grad_normed_two)
    grad_middle = grad_out.astype(jnp.float32) + middle_part
    grad_one = grad_middle.astype(jnp.bfloat16)
    out_weight_grad = jnp.einsum(
        "rd,re->de", attended, grad_one, preferred_element_type=jnp.float32
    )
    out_bias_grad = jnp.sum(grad_one.astype(jnp.float32), axis=0)
    grad_attended = jnp.einsum(
        "re,de->rd", grad_one, full_out, preferred_element_type=jnp.float32
    ).astype(jnp.bfloat16)
    score_scale = 1.0 / math.sqrt(HEAD_DIM)
    split_grad = grad_attended.reshape(row_count, HEADS, HEAD_DIM)
    query_pieces = []
    key_pieces = []
    value_pieces = []
    for first_head in range(0, HEADS, 4):
        head_queries = split_queries[:, first_head : first_head + 4]
        head_keys = split_keys[:, first_head : first_head + 4]
        head_values = split_values[:, first_head : first_head + 4]
        head_grad = split_grad[:, first_head : first_head + 4]
        head_probs = group_probs(head_queries, head_keys, key_valid, score_scale)
        low_probs = head_probs.astype(jnp.bfloat16)
        value_term = jnp.einsum(
            "gqk,qgd->kgd", low_probs, head_grad, preferred_element_type=jnp.float32
        )
        value_pieces.append(value_term.reshape(key_count, 4 * HEAD_DIM))
        grad_probs = jnp.einsum(
            "qgd,kgd->gqk", head_grad, head_values, preferred_element_type=jnp.float32
        )
        inner_sum = jnp.sum(head_probs * grad_probs, axis=-1, keepdims=True)
        grad_scores = (head_probs * (grad_probs - inner_sum)).astype(jnp.bfloat16)
        query_term = (
            jnp.einsum("gqk,kgd->qgd", grad_scores, head_keys, preferred_element_type=jnp.float32)
            * score_scale
        )
        query_pieces.append(query_term.reshape(row_count, 4 * HEAD_DIM))
        key_term = (
            jnp.einsum(
                "gqk,qgd->kgd", grad_scores, head_queries, preferred_element_type=jnp.float32
            )
            * score_scale
        )
        key_pieces.append(key_term.reshape(key_count, 4 * HEAD_DIM))
    key_part = jnp.concatenate(key_pieces, axis=1)
    value_part = jnp.concatenate(value_pieces, axis=1)
    key_sum, value_sum = (
        lax.psum_scatter(
            key_part.astype(jnp.bfloat16), "seq", scatter_dimension=0, tiled=True
        ).astype(jnp.float32),
        lax.psum_scatter(
            value_part.astype(jnp.bfloat16), "seq", scatter_dimension=0, tiled=True
        ).astype(jnp.float32),
    )
    grad_queries = jnp.concatenate(query_pieces, axis=1).astype(jnp.bfloat16)
    grad_qkv = jnp.concatenate(
        [grad_queries, key_sum.astype(jnp.bfloat16), value_sum.astype(jnp.bfloat16)], axis=1
    )
    qkv_weight_grad = jnp.einsum("rd,re->de", normed, grad_qkv, preferred_element_type=jnp.float32)
    column_sums = jnp.sum(grad_qkv.astype(jnp.float32), axis=0)
    query_bias_grad = column_sums[:model_width]
    value_bias_grad = column_sums[2 * model_width :]
    grad_normed = jnp.einsum("re,de->rd", grad_qkv, full_qkv, preferred_element_type=jnp.float32)
    first_value, first_back = jax.vjp(
        layer_norm, start_sum, full_gain_one.astype(jnp.float32), full_shift_one.astype(jnp.float32)
    )
    start_part, first_gain_grad, first_shift_grad = first_back(grad_normed)
    grad_start = grad_middle + start_part
    tokens_grad = grad_start.astype(jnp.bfloat16)[None]
    lead_bias_grad = jnp.sum(grad_start, axis=0)
    lead_weight_grad = lead_scaled * lead_bias_grad
    owned = (
        lax.psum_scatter(first_gain_grad, ("dp", "seq"), scatter_dimension=0, tiled=True),
        lax.psum_scatter(first_shift_grad, ("dp", "seq"), scatter_dimension=0, tiled=True),
        lax.psum_scatter(qkv_weight_grad, ("dp", "seq"), scatter_dimension=0, tiled=True),
        lax.psum_scatter(query_bias_grad, ("dp", "seq"), scatter_dimension=0, tiled=True),
        lax.psum_scatter(value_bias_grad, ("dp", "seq"), scatter_dimension=0, tiled=True),
        lax.psum_scatter(out_weight_grad, ("dp", "seq"), scatter_dimension=0, tiled=True),
        lax.psum_scatter(out_bias_grad, ("dp", "seq"), scatter_dimension=0, tiled=True),
        lax.psum_scatter(second_gain_grad, ("dp", "seq"), scatter_dimension=0, tiled=True),
        lax.psum_scatter(second_shift_grad, ("dp", "seq"), scatter_dimension=0, tiled=True),
        lax.psum_scatter(up_weight_grad, ("dp", "seq"), scatter_dimension=0, tiled=True),
        lax.psum_scatter(up_bias_grad, ("dp", "seq"), scatter_dimension=0, tiled=True),
        lax.psum_scatter(down_weight_grad, ("dp", "seq"), scatter_dimension=0, tiled=True),
        lax.psum_scatter(down_bias_grad, ("dp", "seq"), scatter_dimension=0, tiled=True),
        lax.psum_scatter(lead_weight_grad, ("dp", "seq"), scatter_dimension=0, tiled=True),
        lax.psum_scatter(lead_bias_grad, ("dp", "seq"), scatter_dimension=0, tiled=True),
    )
    return (
        block_out[None],
        tokens_grad,
        owned[0],
        owned[1],
        owned[2],
        owned[3],
        owned[4],
        owned[5],
        owned[6],
        owned[7],
        owned[8],
        owned[9],
        owned[10],
        owned[11],
        owned[12],
        owned[13],
        owned[14],
    )


def solution(mesh):
    placed = (
        P("dp", "seq", None),
        P("dp"),
        P("dp"),
        P("dp", "seq"),
        P(("dp", "seq")),
        P(("dp", "seq")),
        P(("dp", "seq"), None),
        P(("dp", "seq")),
        P(("dp", "seq")),
        P(("dp", "seq"), None),
        P(("dp", "seq")),
        P(("dp", "seq")),
        P(("dp", "seq")),
        P(("dp", "seq"), None),
        P(("dp", "seq")),
        P(("dp", "seq"), None),
        P(("dp", "seq")),
        P(("dp", "seq")),
        P(("dp", "seq")),
        P("dp", "seq", None),
    )
    return jax.shard_map(
        body,
        mesh=mesh,
        in_specs=placed,
        out_specs=(
            P("dp", "seq", None),
            P("dp", "seq", None),
            P(("dp", "seq")),
            P(("dp", "seq")),
            P(("dp", "seq"), None),
            P(("dp", "seq")),
            P(("dp", "seq")),
            P(("dp", "seq"), None),
            P(("dp", "seq")),
            P(("dp", "seq")),
            P(("dp", "seq")),
            P(("dp", "seq"), None),
            P(("dp", "seq")),
            P(("dp", "seq"), None),
            P(("dp", "seq")),
            P(("dp", "seq")),
            P(("dp", "seq")),
        ),
        check_vma=False,
    )
```

profile of v0, /device:TPU:14, one launch (start us, length us, event | category | flops | bytes accessed | tf_op | source)
XLA Modules:
  0.0 1146.2 jit_solution(12173013530353247756)
XLA Ops:
  17.0 41.9 %all-reduce.22 = (bf16[1024]{0:T(1024)(128)(2,1)S(1)}, bf16[1024]{0:T(1024)(128)(2,1)S(1)}, bf16[1024]{0:T(1024)(128)(2,1)S(1)}, bf16[1024]{0:T(1024)(128)(2,1)S...) all-reduce(bf16[1024]{0:T(1024)(128)(2,1)S(1)} %dynamic-update-slic, ...), channel_id=1, replica_groups=mesh['dp'=8,'seq'=4] {'dp','seq'}, use_global_device_ids=true, to_apply=%add.6 | all-reduce | flops 10240 | bytes 40960
  62.3 18.6 %all-gather.8.cloned.1.call-done = bf16[1024,3072]{1,0:T(8,128)(2,1)} async-done(((bf16[32,3072]{1,0:T(8,128)(2,1)}), bf16[1024,3072]{1,0:T(8,128)(2,1)}) %all-gather.8.cloned.1.call-update) | async-done | bytes 6291472 | tf_op jit(solution)/shard_map/all_gather | solution.py:44
  80.8 4.9 fusion.96
  90.5 28.9 %all-gather = bf16[32,1,128]{2,1,0:T(2,128)(2,1)S(1)} all-gather(bf16[1,1,128]{2,1,0:T(2,128)(2,1)S(1)} %bitcast.200), channel_id=1, replica_groups=mesh['dp'=8,'seq'=4] {'dp','seq'}, dimensions={0}, use_global_device_ids=true | all-gather | bytes 8448 | tf_op jit(solution)/shard_map/all_gather | solution.py:52
  120.9 4.2 copy.57
  125.1 8.4 all-gather.12.cloned.1.call-done
  133.4 2.9 copy.59
  149.9 42.0 %all-gather.14.cloned.1.call-done = bf16[1024,1024]{1,0:T(8,128)(2,1)} async-done(((bf16[32,1024]{1,0:T(8,128)(2,1)}), bf16[1024,1024]{1,0:T(8,128)(2,1)}) %all-gather.14.cloned.1.call-update) | async-done | bytes 2097168 | tf_op jit(solution)/shard_map/all_gather | solution.py:47
  194.6 77.0 %all-gather.16.cloned.1.call-done = bf16[1024,4096]{1,0:T(8,128)(2,1)} async-done(((bf16[32,4096]{1,0:T(8,128)(2,1)}), bf16[1024,4096]{1,0:T(8,128)(2,1)}) %all-gather.16.cloned.1.call-update) | async-done | bytes 8388624 | tf_op jit(solution)/shard_map/all_gather | solution.py:51
  271.6 16.4 %multiply_convert_fusion.4 = (bf16[256,4096]{1,0:T(8,128)(2,1)}, f32[256,4096]{1,0:T(8,128)}, f32[256,4096]{1,0:T(8,128)}) fusion(f32[4096]{0:T(1024)S(1)} %bitcast.198, bf16[1024,4096]{1,0:T(8,128)(2,1)} %all-gather.16.cloned.1.call-done, f32[256,1024]{1,0:T(8,128)S(1)} %get-tuple-element.67, f32[1024]{0:T(1024)S(1)} %convert_element_type.182, ...), kind=kOutput, calls=%fused_computation.17 | convolution fusion | flops 2218000384 | bytes 19949568 | tf_op jit(solution)/shard_map/dot_general | solution.py:139
  288.0 62.4 %all-gather.18.cloned.1.call-done = bf16[4096,1024]{1,0:T(8,128)(2,1)} async-done(((bf16[128,1024]{1,0:T(8,128)(2,1)}), bf16[4096,1024]{1,0:T(8,128)(2,1)}) %all-gather.18.cloned.1.call-update) | async-done | bytes 8388624 | tf_op jit(solution)/shard_map/all_gather | solution.py:53
  350.4 11.7 %convert_reduce_fusion = (f32[4096]{0:T(1024)S(1)}, bf16[256,4096]{1,0:T(8,128)(2,1)S(1)}) fusion(f32[256,4096]{1,0:T(8,128)} %get-tuple-element.52, f32[256,4096]{1,0:T(8,128)} %get-tuple-element.68, bf16[4096,1024]{1,0:T(8,128)(2,1)} %all-gather.18.cloned.1.call-done, bf16[1,256,1024]{2,1,0:T(8,128)(2,1)S(1)} %copy-done.1, f32[256]{0:T(256)S(1)} %fusion.81), kind=kOutput, calls=%fused_computation.7 | convolution fusion | flops 2165043200 | bytes 19416064 | tf_op jit(solution)/shard_map/rd,fd->rf/dot_general | solution.py:255
  362.2 2.7 multiply_reduce_fusion.4
  370.1 5.4 multiply_reduce_fusion
  375.5 3.1 multiply_reduce_fusion.1
  382.9 4.2 multiply_convert_fusion
  389.2 2.9 multiply_convert_fusion.1
  397.7 3.1 convolution_convert_fusion
  408.8 4.0 fusion.80
  412.9 2.7 fusion.34
  420.6 7.1 reduce-scatter.7.cloned.1.call-done
  429.6 32.3 %reduce-scatter.9.cloned.1.call-done = bf16[256,1024]{0,1:T(8,128)(2,1)} async-done(((bf16[1024,1024]{0,1:T(8,128)(2,1)}), bf16[256,1024]{0,1:T(8,128)(2,1)}) %reduce-scatter.9.cloned.1.call-update) | async-done | bytes 524304 | tf_op jit(solution)/shard_map/reduce_scatter | solution.py:315
  463.8 8.0 fusion.94
  471.9 9.8 fusion.99
  482.0 9.8 fusion.100
  492.5 7.2 fusion.33
  501.6 5.3 fusion.106
  509.0 42.6 %all-reduce.21 = (f32[1024]{0:T(1024)S(1)}, f32[1024]{0:T(1024)S(1)}, f32[1024]{0:T(1024)S(1)}, f32[1024]{0:T(1024)S(1)}, f32[1024]{0:T(1024)S(1)}, /*index=5*/f...) all-reduce(f32[1024]{0:T(1024)S(1)} %get-tuple-element.19, ...), channel_id=4, replica_groups=mesh['dp'=8,'seq'=4] {'dp','seq'}, use_global_device_ids=true, to_apply=%region_23.24.clone | all-reduce | flops 14336 | bytes 114688
  558.1 16.1 %reduce-scatter.13.cloned.1.call-done = f32[32,1024]{1,0:T(8,128)} async-done(((f32[1024,1024]{1,0:T(8,128)}), f32[32,1024]{1,0:T(8,128)}) %reduce-scatter.13.cloned.1.call-update) | async-done | bytes 131088 | tf_op jit(solution)/shard_map/reduce_scatter | solution.py:342
  574.1 190.1 %reduce-scatter.11.cloned.1.call-done = f32[32,3072]{1,0:T(8,128)} async-done(((f32[1024,3072]{1,0:T(8,128)}), f32[32,3072]{1,0:T(8,128)}) %reduce-scatter.11.cloned.1.call-update) | async-done | bytes 393232 | tf_op jit(solution)/shard_map/reduce_scatter | solution.py:339
  764.2 187.4 %reduce-scatter.15.cloned.1.call-done = f32[32,4096]{1,0:T(8,128)} async-done(((f32[1024,4096]{1,0:T(8,128)}), f32[32,4096]{1,0:T(8,128)}) %reduce-scatter.15.cloned.1.call-update) | async-done | bytes 524304 | tf_op jit(solution)/shard_map/reduce_scatter | solution.py:346
  951.6 187.3 %reduce-scatter.17.cloned.1.call-done = f32[128,1024]{1,0:T(8,128)} async-done(((f32[4096,1024]{1,0:T(8,128)}), f32[128,1024]{1,0:T(8,128)}) %reduce-scatter.17.cloned.1.call-update) | async-done | bytes 524304 | tf_op jit(solution)/shard_map/reduce_scatter | solution.py:348
  (218 shorter events, 79.3 us)
Async XLA Ops:
  7.2 73.6 %all-gather.8.cloned.1.call-start = ((), (), s32[]{:S(2)}) async-start(), calls=%async_computation.6 | async-start | bytes 6488064 | tf_op jit(solution)/shard_map/all_gather | solution.py:44
  7.9 112.9 %all-gather.10.cloned.1.call-start = ((), (), s32[]{:S(2)}) async-start(), calls=%async_computation.7 | async-start | bytes 2621440 | tf_op jit(solution)/shard_map/all_gather | solution.py:107
  59.0 26.8 %copy-start.29 = (f32[1024]{0:T(1024)}, f32[1024]{0:T(1024)S(1)}, u32[]{:S(2)}) copy-start(f32[1024]{0:T(1024)S(1)} %convert_element_type.169) | copy-start | bytes 12292
  59.0 26.7 %copy-start.33 = (f32[1024]{0:T(1024)}, f32[1024]{0:T(1024)S(1)}, u32[]{:S(2)}) copy-start(f32[1024]{0:T(1024)S(1)} %convert_element_type.170) | copy-start | bytes 12292
  60.3 25.4 %copy-start.35 = (f32[256]{0:T(256)}, f32[256]{0:T(256)S(1)}, u32[]{:S(2)}) copy-start(f32[256]{0:T(256)S(1)} %broadcast_multiply_fusion.2) | copy-start | bytes 3076
  62.2 23.5 %copy-start.37 = (f32[256]{0:T(256)}, f32[256]{0:T(256)S(1)}, u32[]{:S(2)}) copy-start(f32[256]{0:T(256)S(1)} %fusion.82) | copy-start | bytes 3076
  85.8 33.6 %copy-start.42 = (s32[1,256]{1,0:T(1,128)S(1)}, s32[1,256]{1,0:T(1,128)}, u32[]{:S(2)}) copy-start(s32[1,256]{1,0:T(1,128)} %param.23) | copy-start | bytes 3076
  87.0 46.4 %all-gather.12.cloned.1.call-start = ((), (), s32[]{:S(2)}) async-start(), calls=%async_computation.8 | async-start | bytes 2621440 | tf_op jit(solution)/shard_map/all_gather | solution.py:106
  88.0 103.9 %all-gather.14.cloned.1.call-start = ((), (), s32[]{:S(2)}) async-start(), calls=%async_computation.9 | async-start | bytes 2162688 | tf_op jit(solution)/shard_map/all_gather | solution.py:47
  88.6 183.0 %all-gather.16.cloned.1.call-start = ((), (), s32[]{:S(2)}) async-start(), calls=%async_computation.10 | async-start | bytes 8650752 | tf_op jit(solution)/shard_map/all_gather | solution.py:51
  89.2 261.2 %all-gather.18.cloned.1.call-start = ((), (), s32[]{:S(2)}) async-start(), calls=%async_computation.11 | async-start | bytes 8650752 | tf_op jit(solution)/shard_map/all_gather | solution.py:53
  89.7 338.0 %reduce-scatter.7.cloned.1.call-start = ((), (), s32[]{:S(2)}) async-start(), calls=%async_computation.12 | async-start | bytes 2621440 | tf_op jit(solution)/shard_map/reduce_scatter | solution.py:312
  120.8 17.7 %copy-start.25 = (bf16[256,1024]{0,1:T(8,128)(2,1)}, bf16[256,1024]{0,1:T(8,128)(2,1)S(1)}, u32[]{:S(2)}) copy-start(bf16[256,1024]{0,1:T(8,128)(2,1)S(1)} %copy.58) | copy-start | bytes 1572868
  142.1 5.3 copy-start.4
  149.0 42.8 %copy-start.31 = (bf16[4,64,256]{2,1,0:T(8,128)(2,1)}, bf16[4,64,256]{2,1,0:T(8,128)(2,1)S(1)}, u32[]{:S(2)}) copy-start(bf16[4,64,256]{2,1,0:T(8,128)(2,1)S(1)} %convolution_convert_fusion.7) | copy-start | bytes 393220
  149.0 42.8 %copy-start = (bf16[1,256,1024]{2,1,0:T(8,128)(2,1)S(1)}, bf16[1,256,1024]{2,1,0:T(8,128)(2,1)}, u32[]{:S(2)}) copy-start(bf16[1,256,1024]{2,1,0:T(8,128)(2,1)} %param.20) | copy-start | bytes 1572868
  149.9 121.7 %copy-start.32 = (bf16[4,64,256]{2,1,0:T(8,128)(2,1)}, bf16[4,64,256]{2,1,0:T(8,128)(2,1)S(1)}, u32[]{:S(2)}) copy-start(bf16[4,64,256]{2,1,0:T(8,128)(2,1)S(1)} %convolution_convert_fusion.8) | copy-start | bytes 393220
  271.6 78.8 %copy-start.1 = (bf16[1,256,1024]{2,1,0:T(8,128)(2,1)S(1)}, bf16[1,256,1024]{2,1,0:T(8,128)(2,1)}, u32[]{:S(2)}) copy-start(bf16[1,256,1024]{2,1,0:T(8,128)(2,1)} %param.39) | copy-start | bytes 1572868
  350.4 11.8 %copy-start.44 = (bf16[1024,4096]{1,0:T(8,128)(2,1)S(1)}, bf16[1024,4096]{1,0:T(8,128)(2,1)}, u32[]{:S(2)}) copy-start(bf16[1024,4096]{1,0:T(8,128)(2,1)} %all-gather.16.cloned.1.call-done) | copy-start | bytes 25165828
  370.0 5.4 copy-start.5
  370.0 5.4 copy-start.17
  370.0 5.4 copy-start.27
  397.6 64.3 %reduce-scatter.9.cloned.1.call-start = ((), (), s32[]{:S(2)}) async-start(), calls=%async_computation.13 | async-start | bytes 2621440 | tf_op jit(solution)/shard_map/reduce_scatter | solution.py:315
  408.8 165.3 %reduce-scatter.13.cloned.1.call-start = ((), (), s32[]{:S(2)}) async-start(), calls=%async_computation.15 | async-start | bytes 4325376 | tf_op jit(solution)/shard_map/reduce_scatter | solution.py:342
  412.8 351.3 %reduce-scatter.11.cloned.1.call-start = ((), (), s32[]{:S(2)}) async-start(), calls=%async_computation.14 | async-start | bytes 12976128 | tf_op jit(solution)/shard_map/reduce_scatter | solution.py:339
  418.5 45.3 %copy-start.30 = (f32[1024]{0:T(1024)S(1)}, f32[1024]{0:T(1024)}, u32[]{:S(2)}) copy-start(f32[1024]{0:T(1024)} %copy-done.29) | copy-start | bytes 12292
  418.5 45.3 %copy-start.34 = (f32[1024]{0:T(1024)S(1)}, f32[1024]{0:T(1024)}, u32[]{:S(2)}) copy-start(f32[1024]{0:T(1024)} %copy-done.33) | copy-start | bytes 12292
  418.5 45.3 %copy-start.36 = (f32[256]{0:T(256)S(1)}, f32[256]{0:T(256)}, u32[]{:S(2)}) copy-start(f32[256]{0:T(256)} %copy-done.35) | copy-start | bytes 3076
  418.5 45.3 %copy-start.38 = (f32[256]{0:T(256)S(1)}, f32[256]{0:T(256)}, u32[]{:S(2)}) copy-start(f32[256]{0:T(256)} %copy-done.37) | copy-start | bytes 3076
  471.8 479.8 %reduce-scatter.15.cloned.1.call-start = ((), (), s32[]{:S(2)}) async-start(), calls=%async_computation.16 | async-start | bytes 17301504 | tf_op jit(solution)/shard_map/reduce_scatter | solution.py:346
  481.7 657.2 %reduce-scatter.17.cloned.1.call-start = ((), (), s32[]{:S(2)}) async-start(), calls=%async_computation.17 | async-start | bytes 17301504 | tf_op jit(solution)/shard_map/reduce_scatter | solution.py:348
  501.6 5.4 copy-start.40
  (26 other events, 68.6 us)
Sparse Core Ops, SparseCore 0:
  10.9 69.8 all-gather.7
  87.2 21.4 all-gather.9
  110.8 22.5 all-gather.11
  136.1 55.6 all-gather.13
  194.6 76.9 all-gather.15
  274.3 76.0 all-gather.17
  397.8 29.9 reduce-scatter.6
  430.4 31.4 reduce-scatter.8
  464.8 109.2 reduce-scatter.12
  580.6 183.5 reduce-scatter.10
  767.2 184.3 reduce-scatter.14
  954.4 184.4 reduce-scatter.16
where the time goes:
time: 1150 us
  waiting for transfers between devices  831 us (72%)
  matrix products  115 us (10%)
  blocking collectives  113 us (10%)
  local copies, waits for them, and re-layouts  43.6 us (4%)
  other arithmetic  25.7 us (2%)
  between operations  16.7 us (1%)
    reduce_scatter x1, waiting for transfers between devices, body(): lax.psum_scatter(qkv_weight_grad, ('dp', 'seq'), scatter_dimension=0, til...  190 us
    reduce_scatter x1, waiting for transfers between devices, body(): lax.psum_scatter(up_weight_grad, ('dp', 'seq'), scatter_dimension=0, tile...  187 us
    reduce_scatter x1, waiting for transfers between devices, body(): lax.psum_scatter(down_weight_grad, ('dp', 'seq'), scatter_dimension=0, ti...  187 us
    unnamed x2, blocking collectives  84.6 us
    all_gather x1, waiting for transfers between devices, collect_weights(): lax.all_gather(up_weight, ('dp', 'seq'), axis=0, tiled=True)  77 us
    all_gather x1, waiting for transfers between devices, collect_weights(): lax.all_gather(down_weight, ('dp', 'seq'), axis=0, tiled=True)  62.4 us
    all_gather x1, waiting for transfers between devices, collect_weights(): lax.all_gather(out_weight, ('dp', 'seq'), axis=0, tiled=True)  42 us
    reduce_scatter x1, waiting for transfers between devices, body(): lax.psum_scatter(value_part.astype(jnp.bfloat16), 'seq', scatter_dimensio...  32.3 us
  transfers between devices with their start and end apart: 12, of which 11 were waited for; matrix products, arithmetic and copies ran while one was open for 11% of the time, Pallas kernels for 0%

commit v1 on v0

v1 whole, which is shorter than its diff:
```python
import math

import jax
import jax.numpy as jnp
from jax import lax
from jax.sharding import PartitionSpec as P

HEADS = 16
HEAD_DIM = 64
EPSILON = 1e-06
MASKED = -1e30
F32 = jnp.float32
BF16 = jnp.bfloat16


def dot(left, right, contract):
    return lax.dot_general(left, right, (contract, ((), ())), preferred_element_type=F32)


def normalise(values):
    centered = values - jnp.mean(values, axis=-1, keepdims=True)
    rate = lax.rsqrt(jnp.mean(centered * centered, axis=-1, keepdims=True) + EPSILON)
    return centered * rate, rate


def norm_back(upstream, xhat, rate, gain):
    scaled = upstream * gain
    inner = jnp.mean(scaled * xhat, axis=-1, keepdims=True)
    return rate * (scaled - jnp.mean(scaled, axis=-1, keepdims=True) - xhat * inner)


def swap(values, bit, size):
    return lax.ppermute(values, "seq", [(i, i ^ bit) for i in range(size)])


def far_bits(size):
    bits, bit = [], 2
    while bit < size:
        bits.append(bit)
        bit *= 2
    return bits


def gather_seq(own, size):
    me = lax.axis_index("seq")
    held = [(0, own)]
    for bit in far_bits(size):
        held = held + [(mask ^ bit, swap(piece, bit, size)) for mask, piece in held]
    if size > 1:
        held = held + [(mask ^ 1, swap(piece, 1, size)) for mask, piece in held]
    out = jnp.zeros((size,) + own.shape, own.dtype)
    for mask, piece in held:
        out = lax.dynamic_update_index_in_dim(out, piece, me ^ mask, 0)
    return out


def scatter_seq(terms, size):
    me = lax.axis_index("seq")
    bits = ([1] if size > 1 else []) + far_bits(size)
    masks = list(range(size))
    held = {mask: lax.dynamic_index_in_dim(terms, me ^ mask, 0, keepdims=False) for mask in masks}
    for bit in bits:
        kept = {}
        for mask in sorted(held):
            if mask & bit:
                continue
            kept[mask] = held[mask] + swap(held[mask ^ bit].astype(BF16), bit, size).astype(F32)
        held = kept
    return held[0]


def exchange_seq(blocks, size):
    me = lax.axis_index("seq")
    out = lax.dynamic_update_index_in_dim(
        jnp.zeros_like(blocks), lax.dynamic_index_in_dim(blocks, me, 0, keepdims=False), me, 0
    )
    for mask in range(1, size):
        sent = lax.dynamic_index_in_dim(blocks, me ^ mask, 0, keepdims=False)
        out = lax.dynamic_update_index_in_dim(out, swap(sent, mask, size), me ^ mask, 0)
    return out


def gather_dp(own):
    return lax.all_gather(own, "dp", axis=0, tiled=False)


def scatter_dp(terms):
    return lax.psum_scatter(terms.astype(BF16), "dp", scatter_dimension=0, tiled=False).astype(F32)


def gelu(values):
    return jax.nn.gelu(values, approximate=False)


def head_probs(queries, keys, key_valid):
    scores = dot(queries, keys, ((1,), (1,))) * (1.0 / math.sqrt(HEAD_DIM))
    scores = jnp.where(key_valid[None, :], scores, MASKED)
    weights = jnp.exp(scores - jnp.max(scores, axis=-1, keepdims=True))
    return weights / jnp.sum(weights, axis=-1, keepdims=True)


def make_body(n_dp, n_seq):
    def body(
        tokens,
        lead_hours,
        valid_counts,
        patch_mask,
        first_gain,
        first_shift,
        qkv_weight,
        query_bias,
        value_bias,
        out_weight,
        out_bias,
        second_gain,
        second_shift,
        up_weight,
        up_bias,
        down_weight,
        down_bias,
        lead_weight,
        lead_bias,
        cotangent,
    ):
        me = lax.axis_index("seq")
        rows, width = tokens.shape[1], tokens.shape[2]
        length = rows * n_seq
        part = qkv_weight.shape[0]
        ff_part = down_weight.shape[0]
        ff = up_weight.shape[1]
        cols = width // n_seq
        ff_cols = ff // n_seq
        heads = HEADS // n_seq
        lead = lead_hours[0].astype(F32) / 100.0
        key_valid = jnp.arange(length, dtype=jnp.int32) < valid_counts[0]
        positions = me * rows + jnp.arange(rows, dtype=jnp.int32)
        loss_weight = (patch_mask[0] * (positions < valid_counts[0]).astype(jnp.int32)).astype(BF16)

        small = jnp.concatenate(
            [
                first_gain,
                first_shift,
                query_bias,
                value_bias,
                out_bias,
                second_gain,
                second_shift,
                down_bias,
                lead_weight,
                lead_bias,
                up_bias,
            ]
        )
        tokens_all = gather_seq(tokens[0], n_seq).reshape(length, width)
        small_all = lax.all_gather(small, ("dp", "seq"), axis=0).astype(F32)
        vector = [small_all[:, i * part : (i + 1) * part].reshape(width) for i in range(10)]
        gain_one, shift_one, q_bias, v_bias, o_bias, gain_two, shift_two, d_bias, l_weight, l_bias = vector
        u_bias = lax.dynamic_index_in_dim(
            small_all[:, 10 * part :].reshape(n_dp, n_seq, ff_part), me, 1, keepdims=False
        ).reshape(ff_cols)
        q_bias = lax.dynamic_slice_in_dim(q_bias, me * cols, cols)
        v_bias = lax.dynamic_slice_in_dim(v_bias, me * cols, cols)

        qkv_blocks = jnp.moveaxis(qkv_weight.reshape(part, 3, n_seq, cols), 2, 0).reshape(n_seq, part, 3 * cols)
        up_blocks = jnp.moveaxis(up_weight.reshape(part, n_dp, n_seq, ff_part), 2, 0).reshape(n_seq, part, ff_cols)
        mixed = exchange_seq(jnp.concatenate([qkv_blocks, up_blocks], axis=2), n_seq)
        mixed = mixed.reshape(n_seq * part, 3 * cols + ff_cols)
        qkv = gather_dp(mixed[:, : 3 * cols]).reshape(width, 3 * cols)
        out_rows = gather_dp(out_weight)
        out_full = jnp.moveaxis(gather_seq(out_rows, n_seq), 0, 1).reshape(width, width)
        up = gather_dp(mixed[:, 3 * cols :]).reshape(width, ff_cols)
        down = gather_dp(down_weight).reshape(ff_cols, width)
        grad_out_own = cotangent[0] * loss_weight[:, None]
        grad_out = gather_seq(grad_out_own, n_seq).reshape(length, width)

        start_sum = tokens_all.astype(F32) + lead * l_weight + l_bias
        xhat_one, rate_one = normalise(start_sum)
        normed = (xhat_one * gain_one + shift_one).astype(BF16)
        projected = dot(normed, qkv, ((1,), (0,)))
        queries = (projected[:, :cols] + q_bias).astype(BF16)
        keys = projected[:, cols : 2 * cols].astype(BF16)
        values = (projected[:, 2 * cols :] + v_bias).astype(BF16)
        split = [slice(i * HEAD_DIM, (i + 1) * HEAD_DIM) for i in range(heads)]
        pieces = []
        for piece in split:
            probs = head_probs(queries[:, piece], keys[:, piece], key_valid)
            pieces.append(dot(probs.astype(BF16), values[:, piece], ((1,), (0,))).astype(BF16))
        attended_own = jnp.concatenate(pieces, axis=1)
        attended = jnp.moveaxis(gather_seq(attended_own, n_seq), 0, 1).reshape(length, width)
        middle = start_sum + (dot(attended, out_full, ((1,), (0,))) + o_bias)
        xhat_two, rate_two = normalise(middle)
        normed_two = (xhat_two * gain_two + shift_two).astype(BF16)
        hidden_pre = dot(normed_two, up, ((1,), (0,))) + u_bias
        hidden, gelu_back = jax.vjp(gelu, hidden_pre)
        hidden = hidden.astype(BF16)

        def own_rows(whole):
            return lax.dynamic_slice_in_dim(whole, me * rows, rows, 0)

        branch = scatter_seq(dot(hidden, down, ((1,), (0,))).reshape(n_seq, rows, width), n_seq)
        middle_own = own_rows(middle)
        block_out = (middle_own + (branch + d_bias)).astype(BF16)

        grad_hidden = dot(grad_out, down, ((1,), (1,)))
        grad_pre = gelu_back(grad_hidden)[0].astype(BF16)
        u_bias_grad = jnp.sum(grad_pre.astype(F32), axis=0)
        down_grad = scatter_dp(dot(hidden, grad_out, ((0,), (0,))).reshape(n_dp, ff_part, width))
        up_grad = scatter_dp(dot(normed_two, grad_pre, ((0,), (0,))).reshape(n_dp, n_seq * part, ff_cols))
        grad_two = scatter_seq(dot(grad_pre, up, ((1,), (1,))).reshape(n_seq, rows, width), n_seq)
        xhat_two_own, rate_two_own = own_rows(xhat_two), own_rows(rate_two)
        gain_two_grad = jnp.sum(grad_two * xhat_two_own, axis=0)
        shift_two_grad = jnp.sum(grad_two, axis=0)
        grad_middle = grad_out_own.astype(F32) + norm_back(grad_two, xhat_two_own, rate_two_own, gain_two)
        grad_one_own = grad_middle.astype(BF16)
        o_bias_grad = jnp.sum(grad_one_own.astype(F32), axis=0)
        d_bias_grad = jnp.sum(grad_out_own.astype(F32), axis=0)
        grad_one = gather_seq(grad_one_own, n_seq).reshape(length, width)
        out_mine = lax.dynamic_slice_in_dim(out_full, me * cols, cols, 0)
        grad_attended = dot(grad_one, out_mine, ((1,), (1,))).astype(BF16)
        out_grad = scatter_dp(dot(attended_own, grad_one, ((0,), (0,))).reshape(n_dp, cols // n_dp, width))
        q_pieces, k_pieces, v_pieces = [], [], []
        scale = 1.0 / math.sqrt(HEAD_DIM)
        for piece in split:
            probs = head_probs(queries[:, piece], keys[:, piece], key_valid)
            upstream = grad_attended[:, piece]
            v_pieces.append(dot(probs.astype(BF16), upstream, ((0,), (0,))).astype(BF16))
            grad_probs = dot(upstream, values[:, piece], ((1,), (1,)))
            inner = jnp.sum(probs * grad_probs, axis=-1, keepdims=True)
            grad_scores = (probs * (grad_probs - inner)).astype(BF16)
            q_pieces.append((dot(grad_scores, keys[:, piece], ((1,), (0,))) * scale).astype(BF16))
            k_pieces.append((dot(grad_scores, queries[:, piece], ((0,), (0,))) * scale).astype(BF16))
        grad_qkv = jnp.concatenate(q_pieces + k_pieces + v_pieces, axis=1)
        grad_first = scatter_seq(dot(grad_qkv, qkv, ((1,), (1,))).reshape(n_seq, rows, width), n_seq)
        qkv_grad = scatter_dp(dot(normed, grad_qkv, ((0,), (0,))).reshape(n_dp, n_seq * part, 3 * cols))
        column_sums = jnp.sum(grad_qkv.astype(F32), axis=0)
        xhat_one_own, rate_one_own = own_rows(xhat_one), own_rows(rate_one)
        gain_one_grad = jnp.sum(grad_first * xhat_one_own, axis=0)
        shift_one_grad = jnp.sum(grad_first, axis=0)
        grad_start = grad_middle + norm_back(grad_first, xhat_one_own, rate_one_own, gain_one)
        tokens_grad = grad_start.astype(BF16)
        l_bias_grad = jnp.sum(grad_start, axis=0)
        l_weight_grad = lead * l_bias_grad

        blocks = jnp.concatenate(
            [qkv_grad.reshape(n_seq, part, 3 * cols), up_grad.reshape(n_seq, part, ff_cols)], axis=2
        )
        blocks = exchange_seq(blocks.astype(BF16), n_seq).astype(F32)
        qkv_weight_grad = jnp.moveaxis(blocks[:, :, : 3 * cols].reshape(n_seq, part, 3, cols), 0, 2).reshape(part, 3 * width)
        up_weight_grad = jnp.moveaxis(
            blocks[:, :, 3 * cols :].reshape(n_seq, part, n_dp, ff_part), 0, 2
        ).reshape(part, ff)
        moves = []
        for dp_at in range(n_dp):
            for seq_at in range(n_seq):
                moves.append((dp_at * n_seq + seq_at, seq_at * n_dp + dp_at))
        out_weight_grad = lax.ppermute(out_grad.astype(BF16), ("dp", "seq"), moves).astype(F32)

        def placed_columns(vec):
            return lax.dynamic_update_slice_in_dim(jnp.zeros((width,), F32), vec, me * cols, 0)

        u_placed = lax.dynamic_update_index_in_dim(
            jnp.zeros((n_dp, n_seq, ff_part), F32), u_bias_grad.reshape(n_dp, ff_part), me, 1
        )
        sums = [
            gain_one_grad,
            shift_one_grad,
            placed_columns(column_sums[:cols]),
            placed_columns(column_sums[2 * cols :]),
            o_bias_grad,
            gain_two_grad,
            shift_two_grad,
            d_bias_grad,
            l_weight_grad,
            l_bias_grad,
        ]
        sums = [value.reshape(n_dp * n_seq, part) for value in sums] + [u_placed.reshape(n_dp * n_seq, ff_part)]
        owned = lax.psum_scatter(jnp.concatenate(sums, axis=1), ("dp", "seq"), scatter_dimension=0, tiled=False)
        owned = [owned[i * part : (i + 1) * part] for i in range(10)] + [owned[10 * part :]]
        return (
            block_out[None],
            tokens_grad[None],
            owned[0],
            owned[1],
            qkv_weight_grad,
            owned[2],
            owned[3],
            out_weight_grad,
            owned[4],
            owned[5],
            owned[6],
            up_weight_grad,
            owned[10],
            down_grad,
            owned[7],
            owned[8],
            owned[9],
        )

    return body


def solution(mesh):
    both = P(("dp", "seq"))
    matrix = P(("dp", "seq"), None)
    tokens = P("dp", "seq", None)
    vectors = dict(
        in_specs=(
            tokens,
            P("dp"),
            P("dp"),
            P("dp", "seq"),
            both,
            both,
            matrix,
            both,
            both,
            matrix,
            both,
            both,
            both,
            matrix,
            both,
            matrix,
            both,
            both,
            both,
            tokens,
        ),
        out_specs=(
            tokens,
            tokens,
            both,
            both,
            matrix,
            both,
            both,
            matrix,
            both,
            both,
            both,
            matrix,
            both,
            matrix,
            both,
            both,
            both,
        ),
    )
    return jax.shard_map(
        make_body(mesh.shape["dp"], mesh.shape["seq"]), mesh=mesh, check_vma=False, **vectors
    )
```

time: 1150 us -> 532 us (0.46)
  waiting for transfers between devices: 831 us -> 111 us
  other arithmetic: 25.7 us -> 75.8 us
  local copies, waits for them, and re-layouts: 43.6 us -> 75.9 us
  starting transfers between devices: 0.73 us -> 19 us
  matrix products: 115 us -> 99.9 us
  blocking collectives: 113 us -> 125 us
    reduce_scatter x6 -> x4, waiting for transfers between devices: 620 us -> 72.6 us  [scatter_dp(): lax.psum_scatter(terms.astype(BF16), 'dp', scatter_dimension=0, tiled=False)]
    all_gather x6 -> x3, waiting for transfers between devices: 208 us -> 0.01 us  [gather_dp(): return lax.all_gather(own, 'dp', axis=0, tiled=False)]
    ppermute x0 -> x31, waiting for transfers between devices: none -> 38.2 us  [the longest x30 38.2 us: swap(): return lax.ppermute(values, 'seq', [(i, i ^ bit) for i in range(size)])]
    convert_element_type x15 -> x11, other arithmetic: 9.67 us -> 36 us  [the longest x2 13.4 us: body(): hidden = hidden.astype(BF16)]
    another operation x0 -> x12, local copies, waits for them, and re-layouts: none -> 19.8 us  [the longest x4 18.9 us: gelu(): return jax.nn.gelu(values, approximate=False)]
    ppermute x0 -> x31, starting transfers between devices: none -> 18.7 us  [the longest x30 15.8 us: swap(): return lax.ppermute(values, 'seq', [(i, i ^ bit) for i in range(size)])]
    unnamed x128 -> x111, local copies, waits for them, and re-layouts: 30.4 us -> 12.1 us
    dot_general x36, matrix products: 115 us -> 99.9 us  [dot(): lax.dot_general(left, right, (contract, ((), ())), preferred_element_type...]
  transfers between devices with their start and end apart: 12 -> 38, of which waited for: 11 -> 12; matrix products, arithmetic and copies ran while one was open for 11% -> 40% of each run, Pallas kernels for 0% -> 0%
where the time goes in v1:
time: 532 us; the launch traced here: 524 us
  blocking collectives  125 us (23%)
  waiting for transfers between devices  111 us (21%)
  matrix products  99.9 us (19%)
  local copies, waits for them, and re-layouts  75.9 us (14%)
  other arithmetic  75.8 us (14%)
  starting transfers between devices  19 us (4%)
  between operations  17 us (3%)
    dot_general x36, matrix products, dot(): lax.dot_general(left, right, (contract, ((), ())), preferred_element_type...  99.9 us
    unnamed x2, blocking collectives  95.9 us
    reduce_scatter x4, waiting for transfers between devices, scatter_dp(): lax.psum_scatter(terms.astype(BF16), 'dp', scatter_dimension=0, tiled=False)  72.6 us
    ppermute x30, waiting for transfers between devices, swap(): return lax.ppermute(values, 'seq', [(i, i ^ bit) for i in range(size)])  38.2 us
    all_gather x1, blocking collectives, gather_dp(): return lax.all_gather(own, 'dp', axis=0, tiled=False)  29.4 us
    another operation x4, local copies, waits for them, and re-layouts, gelu(): return jax.nn.gelu(values, approximate=False)  18.9 us
    ppermute x30, starting transfers between devices, swap(): return lax.ppermute(values, 'seq', [(i, i ^ bit) for i in range(size)])  15.8 us
    another operation x2, other arithmetic, gelu(): return jax.nn.gelu(values, approximate=False)  14.7 us
  transfers between devices with their start and end apart: 38, of which 12 were waited for; matrix products, arithmetic and copies ran while one was open for 40% of the time, Pallas kernels for 0%

profile of v1, /device:TPU:14, one launch (start us, length us, event | category | flops | bytes accessed | tf_op | source)
XLA Modules:
  0.0 523.8 jit_solution(18124660921247990472)
XLA Ops:
  12.6 5.8 %collective-permute-done.4 = bf16[32,1792]{1,0:T(8,128)(2,1)S(1)} collective-permute-done((bf16[32,1792]{1,0:T(8,128)(2,1)S(1)}, bf16[32,1792]{1,0:T(8,128)(2,1)S(1)}, u32[]{:S(2)}, u32[]{:S(2)}) %collective-permute-start.4) | collective-permute-done | bytes 114720 | tf_op jit(solution)/shard_map/ppermute | solution.py:33
  22.0 29.4 %all-gather.2 = bf16[256,1024]{1,0:T(8,128)(2,1)S(1)} all-gather(bf16[32,1024]{1,0:T(8,128)(2,1)S(1)} %copy-done.33), channel_id=4, replica_groups=mesh['dp'=8,'seq'=4] {'dp'}, dimensions={0}, use_global_device_ids=true | all-gather | bytes 589824 | tf_op jit(solution)/shard_map/all_gather | solution.py:84
  55.2 53.2 %all-reduce = bf16[14336]{0:T(1024)(128)(2,1)S(1)} all-reduce(bf16[14336]{0:T(1024)(128)(2,1)S(1)} %dynamic-update-slice), channel_id=2, replica_groups=mesh['dp'=8,'seq'=4] {'dp','seq'}, use_global_device_ids=true, to_apply=%add | all-reduce | flops 14336 | bytes 57344
  127.0 4.0 fusion.149
  136.2 3.7 fusion.21
  152.3 6.5 %collective-permute-done.6 = bf16[1024,256]{0,1:T(8,128)(2,1)S(1)} collective-permute-done((bf16[1024,256]{0,1:T(8,128)(2,1)S(1)}, bf16[1024,256]{0,1:T(8,128)(2,1)S(1)}, u32[]{:S(2)}, u32[]{:S(2)}) %collective-permute-start.6) | collective-permute-done | bytes 524320 | tf_op jit(solution)/shard_map/ppermute | solution.py:33
  160.8 4.6 fusion.150
  169.7 7.1 %fusion.74 = f32[1024,1024]{1,0:T(8,128)} fusion(bf16[1024,1024]{1,0:T(8,128)(2,1)} %all-gather.11.cloned.1.call-done, f32[1024,1024]{1,0:T(8,128)} %subtract_multiply_fusion.1, f32[1024]{0:T(1024)S(1)} %add.297, f32[1024]{0:T(1024)S(1)} %mul.284), kind=kOutput, calls=%fused_computation.177 | convolution fusion | flops 2150629376 | bytes 10493952 | tf_op jit(solution)/shard_map/dot_general | solution.py:17
  176.9 16.1 %convert_reduce_fusion = (f32[1024]{0:T(1024)S(1)}, bf16[1024,1024]{1,0:T(8,128)(2,1)S(1)}, f32[1024,1024]{1,0:T(8,128)}, f32[1024,1024]{0,1:T(8,128)}) fusion(f32[1024,1024]{1,0:T(8,128)} %fusion.74, f32[1024]{0:T(1024)S(1)} %bitcast.289, bf16[1024,1024]{1,0:T(8,128)(2,1)} %bitcast.265, bf16[1024,1024]{1,0:T(8,128)(2,1)} %all-gather.13.cloned.1.call-done), kind=kOutput, calls=%fused_computation.19 | convolution fusion | flops 2226125824 | bytes 18882560 | tf_op jit(solution)/shard_map/dot_general | solution.py:17
  201.1 3.3 fusion.27
  204.3 3.9 copy.112
  208.4 4.7 multiply_convert_fusion.4
  223.0 5.6 %copy.100 = f32[1024,1024]{1,0:T(8,128)} copy(f32[1024,1024]{0,1:T(8,128)} %get-tuple-element.50) | data formatting | bytes 8388608 | tf_op jit(solution)/shard_map/jvp()/mul | solution.py:92
  239.7 6.7 %convolution_convert_fusion.1 = bf16[1024,1024]{1,0:T(8,128)(2,1)} fusion(bf16[1024,1024]{1,0:T(8,128)(2,1)} %copy-done.51, f32[1024,1024]{1,0:T(8,128)} %subtract_multiply_fusion.1, f32[1024]{0:T(1024)S(1)} %add.297, f32[1024]{0:T(1024)S(1)} %mul.284), kind=kOutput, calls=%fused_computation.83 | convolution fusion | flops 2151677952 | bytes 8396800 | tf_op jit(solution)/shard_map/dot_general | solution.py:17
  255.0 3.0 copy-done.3
  258.0 10.1 %multiply_reduce_fusion = (f32[1024]{0:T(1024)S(1)}, f32[1024]{0:T(1024)S(1)}, f32[1024]{0:T(1024)S(1)}, f32[1024]{0:T(1024)S(1)}, f32[1024,1024]{0,1:T(8,128)}) fusion(f32[1024]{0:T(1024)S(1)} %get-tuple-element.35, f32[1024]{0:T(1024)S(1)} %get-tuple-element.32, f32[1024,1024]{0,1:T(8,128)S(1)} %copy-done.1, pred[1024]{0:T(1024)(128)(4,1)S(1)} %iota_compare_fusion, ...), kind=kOutput, calls=%fused_computation.22 | convolution fusion | flops 159379456 | bytes 33866752 | tf_op jit(solution)/shard_map/dot_general | solution.py:17
  268.1 3.4 multiply_convert_fusion.1
  271.5 8.5 %multiply_convert_fusion = (bf16[1024,1024]{0,1:T(8,128)(2,1)S(1)}, bf16[1024,1024]{0,1:T(8,128)(2,1)S(1)}, bf16[1024,1024]{0,1:T(8,128)(2,1)S(1)}) fusion(f32[1024,1024]{0,1:T(8,128)} %get-tuple-element.105, f32[1024]{0:T(1024)S(1)} %get-tuple-element.25, f32[1024]{0:T(1024)S(1)} %get-tuple-element.35, f32[1024]{0:T(1024)S(1)} %get-tuple-element.32, ...), kind=kLoop, calls=%fused_computation.21 | loop fusion | flops 22020096 | bytes 31495168 | tf_op jit(solution)/shard_map/convert_element_type | solution.py:229
  296.3 3.0 convolution_convert_fusion.2
  299.3 11.8 %broadcast_subtract_fusion = (f32[1024,1024]{1,0:T(8,128)}, f32[1024,1024]{1,0:T(8,128)}, f32[1024,1024]{1,0:T(8,128)}) fusion(f32[1024,1024]{1,0:T(8,128)} %copy.100), kind=kLoop, calls=%fused_computation.81 | loop fusion | flops 58720256 | bytes 16777216 | tf_op jit(solution)/shard_map/jvp()/erfc | solution.py:92
  311.1 5.4 %copy.105 = f32[1024,1024]{0,1:T(8,128)} copy(f32[1024,1024]{1,0:T(8,128)} %get-tuple-element.36) | data formatting | bytes 8388608 | tf_op jit(solution)/shard_map/jvp()/erfc | solution.py:92
  316.5 5.5 %copy.106 = f32[1024,1024]{0,1:T(8,128)} copy(f32[1024,1024]{1,0:T(8,128)} %get-tuple-element.37) | data formatting | bytes 8388608 | tf_op jit(solution)/shard_map/jvp()/erfc | solution.py:92
  322.0 5.5 %copy.108 = f32[1024,1024]{0,1:T(8,128)} copy(f32[1024,1024]{1,0:T(8,128)} %get-tuple-element.51) | data formatting | bytes 8388608 | tf_op jit(solution)/shard_map/jvp()/erfc | solution.py:92
  327.4 8.7 %fusion.1 = bf16[1024,1024]{0,1:T(8,128)(2,1)S(1)} fusion(pred[1024,1024]{0,1:T(8,128)(4,1)} %copy.107, f32[1024,1024]{0,1:T(8,128)} %copy.108, f32[1024,1024]{0,1:T(8,128)} %copy.105, f32[1024,1024]{0,1:T(8,128)} %copy.106, f32[1024,1024]{1,0:T(8,128)} %fusion.74, f32[1024]{0:T(1024)S(1)} %bitcast.291), kind=kLoop, calls=%fused_computation.3 | loop fusion | flops 9437184 | bytes 19927040 | tf_op jit(solution)/shard_map/convert_element_type | solution.py:195
  338.7 5.9 %convolution_convert_fusion = bf16[8,128,1024]{2,1,0:T(8,128)(2,1)} fusion(bf16[8,128,1024]{2,1,0:T(8,128)(2,1)} %bitcast.272, bf16[1024,1024,1]{1,0,2:T(8,128)(2,1)} %bitcast.266), kind=kOutput, calls=%fused_computation.82 | convolution fusion | flops 2148532224 | bytes 6291456 | tf_op jit(solution)/shard_map/dot_general | solution.py:17
  350.3 3.7 fusion.33
  357.5 4.2 collective-permute-done.14
  371.9 10.7 %collective-permute-done.26 = bf16[256,1024]{1,0:T(8,128)(2,1)} collective-permute-done((bf16[256,1024]{1,0:T(8,128)(2,1)}, bf16[256,1024]{1,0:T(8,128)(2,1)}, u32[]{:S(2)}, u32[]{:S(2)}) %collective-permute-start.26) | collective-permute-done | bytes 524320 | tf_op jit(solution)/shard_map/ppermute | solution.py:33
  387.6 42.6 %all-reduce.1 = f32[32,448]{1,0:T(8,128)S(1)} all-reduce(f32[32,448]{1,0:T(8,128)S(1)} %concatenate.23), channel_id=7, replica_groups=mesh['dp'=8,'seq'=4] {'dp','seq'}, use_global_device_ids=true, to_apply=%region_29.30.clone | all-reduce | flops 14336 | bytes 114688
  432.1 3.6 reduce-scatter.5.cloned.1.call-done
  436.8 69.1 %reduce-scatter.11.cloned.1.call-done = bf16[1,128,1024]{2,1,0:T(8,128)(2,1)} async-done(((bf16[8,128,1024]{2,1,0:T(8,128)(2,1)}), bf16[1,128,1024]{2,1,0:T(8,128)(2,1)}) %reduce-scatter.11.cloned.1.call-update) | async-done | bytes 262160 | tf_op jit(solution)/shard_map/reduce_scatter | solution.py:88
  508.1 5.6 %collective-permute-done.28 = bf16[32,1792]{1,0:T(8,128)(2,1)S(1)} collective-permute-done((bf16[32,1792]{1,0:T(8,128)(2,1)S(1)}, bf16[32,1792]{1,0:T(8,128)(2,1)S(1)}, u32[]{:S(2)}, u32[]{:S(2)}) %collective-permute-start.28) | collective-permute-done | bytes 114720 | tf_op jit(solution)/shard_map/ppermute | solution.py:33
  (337 shorter events, 142.1 us)
Async XLA Ops:
  7.2 119.8 %all-gather.9.cloned.1.call-start = ((), (), s32[]{:S(2)}) async-start(), calls=%async_computation.8 | async-start | bytes 1769472 | tf_op jit(solution)/shard_map/all_gather | solution.py:84
  10.4 8.0 %collective-permute-start.5 = (bf16[32,1792]{1,0:T(8,128)(2,1)S(1)}, bf16[32,1792]{1,0:T(8,128)(2,1)S(1)}, u32[]{:S(2)}, u32[]{:S(2)}) collective-permute-start(bf16[32,1792]{1,0:T(8,128)(2,1)S(1)} %get-tuple-element.66), channel_id=1, source_target_pairs={{0,3},{1,2},{2,1},{3,0},{4,7},{5,6},{6,5},{7,4},{8,11},{9,10},{10,... | collective-permute-start | bytes 344072 | tf_op jit(solution)/shard_map/ppermute | solution.py:33
  11.0 7.3 %collective-permute-start.4 = (bf16[32,1792]{1,0:T(8,128)(2,1)S(1)}, bf16[32,1792]{1,0:T(8,128)(2,1)S(1)}, u32[]{:S(2)}, u32[]{:S(2)}) collective-permute-start(bf16[32,1792]{1,0:T(8,128)(2,1)S(1)} %get-tuple-element.67), channel_id=1, source_target_pairs={{0,2},{1,3},{2,0},{3,1},{4,6},{5,7},{6,4},{7,5},{8,10},{9,11},{10,... | collective-permute-start | bytes 344072 | tf_op jit(solution)/shard_map/ppermute | solution.py:33
  19.1 150.6 %all-gather.11.cloned.1.call-start = ((), (), s32[]{:S(2)}) async-start(), calls=%async_computation.9 | async-start | bytes 2359296 | tf_op jit(solution)/shard_map/all_gather | solution.py:84
  19.9 156.9 %all-gather.13.cloned.1.call-start = ((), (), s32[]{:S(2)}) async-start(), calls=%async_computation.10 | async-start | bytes 2359296 | tf_op jit(solution)/shard_map/all_gather | solution.py:84
  21.5 98.5 %collective-permute-start.16 = (bf16[256,1024]{1,0:T(8,128)(2,1)S(1)}, bf16[256,1024]{1,0:T(8,128)(2,1)}, u32[]{:S(2)}, u32[]{:S(2)}) collective-permute-start(bf16[256,1024]{1,0:T(8,128)(2,1)S(1)} %get-tuple-element.44), channel_id=1, source_target_pairs={{0,1},{1,0},{2,3},{3,2},{4,5},{5,4},{6,7},{7,6},{8,9},{9,8},{10,11... | collective-permute-start | bytes 1572872 | tf_op jit(solution)/shard_map/ppermute | solution.py:33
  21.5 93.1 %collective-permute-start.15 = (bf16[256,1024]{1,0:T(8,128)(2,1)S(1)}, bf16[256,1024]{1,0:T(8,128)(2,1)}, u32[]{:S(2)}, u32[]{:S(2)}) collective-permute-start(bf16[256,1024]{1,0:T(8,128)(2,1)S(1)} %get-tuple-element.44), channel_id=1, source_target_pairs={{0,2},{1,3},{2,0},{3,1},{4,6},{5,7},{6,4},{7,5},{8,10},{9,11},{10,... | collective-permute-start | bytes 1572872 | tf_op jit(solution)/shard_map/ppermute | solution.py:33
  51.4 66.6 %collective-permute-start.9 = (bf16[8,32,1024]{2,1,0:T(8,128)(2,1)S(1)}, bf16[8,32,1024]{2,1,0:T(8,128)(2,1)}, u32[]{:S(2)}, u32[]{:S(2)}) collective-permute-start(bf16[8,32,1024]{2,1,0:T(8,128)(2,1)S(1)} %bitcast.273), channel_id=1, source_target_pairs={{0,2},{1,3},{2,0},{3,1},{4,6},{5,7},{6,4},{7,5},{8,10},{9,11},{10,... | collective-permute-start | bytes 1572872 | tf_op jit(solution)/shard_map/ppermute | solution.py:33
  54.0 92.7 %collective-permute-start.10 = (bf16[8,32,1024]{2,1,0:T(8,128)(2,1)S(1)}, bf16[8,32,1024]{2,1,0:T(8,128)(2,1)}, u32[]{:S(2)}, u32[]{:S(2)}) collective-permute-start(bf16[8,32,1024]{2,1,0:T(8,128)(2,1)S(1)} %bitcast.274), channel_id=1, source_target_pairs={{0,1},{1,0},{2,3},{3,2},{4,5},{5,4},{6,7},{7,6},{8,9},{9,8},{10,11... | collective-permute-start | bytes 1572872 | tf_op jit(solution)/shard_map/ppermute | solution.py:33
  54.0 62.5 %collective-permute-start = (bf16[256,1024]{1,0:T(8,128)(2,1)}, bf16[256,1024]{1,0:T(8,128)(2,1)}, u32[]{:S(2)}, u32[]{:S(2)}) collective-permute-start(bf16[256,1024]{1,0:T(8,128)(2,1)} %bitcast), channel_id=1, source_target_pairs={{0,2},{1,3},{2,0},{3,1},{4,6},{5,7},{6,4},{7,5},{8,10},{9,11},{10,... | collective-permute-start | bytes 1572872 | tf_op jit(solution)/shard_map/ppermute | solution.py:33
  54.1 314.9 %reduce-scatter.9.cloned.1.call-start = ((), (), s32[]{:S(2)}) async-start(), calls=%async_computation.6 | async-start | bytes 589824 | tf_op jit(solution)/shard_map/reduce_scatter | solution.py:88
  114.5 7.8 %collective-permute-start.1 = (bf16[256,1024]{1,0:T(8,128)(2,1)}, bf16[256,1024]{1,0:T(8,128)(2,1)S(1)}, u32[]{:S(2)}, u32[]{:S(2)}) collective-permute-start(bf16[256,1024]{1,0:T(8,128)(2,1)} %bitcast), channel_id=1, source_target_pairs={{0,1},{1,0},{2,3},{3,2},{4,5},{5,4},{6,7},{7,6},{8,9},{9,8},{10,11... | collective-permute-start | bytes 1572872 | tf_op jit(solution)/shard_map/ppermute | solution.py:33
  116.4 32.2 %collective-permute-start.17 = (bf16[256,1024]{1,0:T(8,128)(2,1)}, bf16[256,1024]{1,0:T(8,128)(2,1)}, u32[]{:S(2)}, u32[]{:S(2)}) collective-permute-start(bf16[256,1024]{1,0:T(8,128)(2,1)} %collective-permute-done.15), channel_id=1, source_target_pairs={{0,1},{1,0},{2,3},{3,2},{4,5},{5,4},{6,7},{7,6},{8,9},{9,8},{10,11... | collective-permute-start | bytes 1572872 | tf_op jit(solution)/shard_map/ppermute | solution.py:33
  120.0 30.5 %collective-permute-start.11 = (bf16[8,32,1024]{2,1,0:T(8,128)(2,1)}, bf16[8,32,1024]{2,1,0:T(8,128)(2,1)}, u32[]{:S(2)}, u32[]{:S(2)}) collective-permute-start(bf16[8,32,1024]{2,1,0:T(8,128)(2,1)} %collective-permute-done.9), channel_id=1, source_target_pairs={{0,1},{1,0},{2,3},{3,2},{4,5},{5,4},{6,7},{7,6},{8,9},{9,8},{10,11... | collective-permute-start | bytes 1572872 | tf_op jit(solution)/shard_map/ppermute | solution.py:33
  144.9 13.9 %collective-permute-start.6 = (bf16[1024,256]{0,1:T(8,128)(2,1)S(1)}, bf16[1024,256]{0,1:T(8,128)(2,1)S(1)}, u32[]{:S(2)}, u32[]{:S(2)}) collective-permute-start(bf16[1024,256]{0,1:T(8,128)(2,1)S(1)} %pad_maximum_fusion), channel_id=1, source_target_pairs={{0,2},{1,3},{2,0},{3,1},{4,6},{5,7},{6,4},{7,5},{8,10},{9,11},{10,... | collective-permute-start | bytes 1572872 | tf_op jit(solution)/shard_map/ppermute | solution.py:33
  150.5 8.7 %collective-permute-start.7 = (bf16[1024,256]{0,1:T(8,128)(2,1)S(1)}, bf16[1024,256]{0,1:T(8,128)(2,1)S(1)}, u32[]{:S(2)}, u32[]{:S(2)}) collective-permute-start(bf16[1024,256]{0,1:T(8,128)(2,1)S(1)} %pad_maximum_fusion), channel_id=1, source_target_pairs={{0,1},{1,0},{2,3},{3,2},{4,5},{5,4},{6,7},{7,6},{8,9},{9,8},{10,11... | collective-permute-start | bytes 1572872 | tf_op jit(solution)/shard_map/ppermute | solution.py:33
  196.6 16.5 %collective-permute-start.18 = (bf16[256,1024]{1,0:T(8,128)(2,1)}, bf16[256,1024]{1,0:T(8,128)(2,1)S(1)}, u32[]{:S(2)}, u32[]{:S(2)}) collective-permute-start(bf16[256,1024]{1,0:T(8,128)(2,1)} %get-tuple-element.54), channel_id=1, source_target_pairs={{0,1},{1,0},{2,3},{3,2},{4,5},{5,4},{6,7},{7,6},{8,9},{9,8},{10,11... | collective-permute-start | bytes 1572872 | tf_op jit(solution)/shard_map/ppermute | solution.py:33
  199.4 14.2 %collective-permute-start.20 = (bf16[256,1024]{1,0:T(8,128)(2,1)}, bf16[256,1024]{1,0:T(8,128)(2,1)S(1)}, u32[]{:S(2)}, u32[]{:S(2)}) collective-permute-start(bf16[256,1024]{1,0:T(8,128)(2,1)} %fusion.59), channel_id=1, source_target_pairs={{0,2},{1,3},{2,0},{3,1},{4,6},{5,7},{6,4},{7,5},{8,10},{9,11},{10,... | collective-permute-start | bytes 1572872 | tf_op jit(solution)/shard_map/ppermute | solution.py:33
  216.0 13.3 %collective-permute-start.21 = (bf16[256,1024]{1,0:T(8,128)(2,1)S(1)}, bf16[256,1024]{1,0:T(8,128)(2,1)S(1)}, u32[]{:S(2)}, u32[]{:S(2)}) collective-permute-start(bf16[256,1024]{1,0:T(8,128)(2,1)S(1)} %get-tuple-element.46), channel_id=1, source_target_pairs={{0,2},{1,3},{2,0},{3,1},{4,6},{5,7},{6,4},{7,5},{8,10},{9,11},{10,... | collective-permute-start | bytes 1572872 | tf_op jit(solution)/shard_map/ppermute | solution.py:33
  219.9 9.7 %collective-permute-start.22 = (bf16[256,1024]{1,0:T(8,128)(2,1)S(1)}, bf16[256,1024]{1,0:T(8,128)(2,1)S(1)}, u32[]{:S(2)}, u32[]{:S(2)}) collective-permute-start(bf16[256,1024]{1,0:T(8,128)(2,1)S(1)} %get-tuple-element.46), channel_id=1, source_target_pairs={{0,1},{1,0},{2,3},{3,2},{4,5},{5,4},{6,7},{7,6},{8,9},{9,8},{10,11... | collective-permute-start | bytes 1572872 | tf_op jit(solution)/shard_map/ppermute | solution.py:33
  223.0 121.7 %collective-permute-start.13 = (bf16[256,1024]{1,0:T(8,128)(2,1)}, bf16[256,1024]{1,0:T(8,128)(2,1)}, u32[]{:S(2)}, u32[]{:S(2)}) collective-permute-start(bf16[256,1024]{1,0:T(8,128)(2,1)} %get-tuple-element.57), channel_id=1, source_target_pairs={{0,1},{1,0},{2,3},{3,2},{4,5},{5,4},{6,7},{7,6},{8,9},{9,8},{10,11... | collective-permute-start | bytes 1572872 | tf_op jit(solution)/shard_map/ppermute | solution.py:33
  234.2 198.0 %reduce-scatter.7.cloned.1.call-start = ((), (), s32[]{:S(2)}) async-start(), calls=%async_computation.5 | async-start | bytes 2359296 | tf_op jit(solution)/shard_map/reduce_scatter | solution.py:88
  246.5 189.2 %reduce-scatter.5.cloned.1.call-start = ((), (), s32[]{:S(2)}) async-start(), calls=%async_computation.4 | async-start | bytes 1769472 | tf_op jit(solution)/shard_map/reduce_scatter | solution.py:88
  299.3 206.6 %reduce-scatter.11.cloned.1.call-start = ((), (), s32[]{:S(2)}) async-start(), calls=%async_computation.7 | async-start | bytes 2359296 | tf_op jit(solution)/shard_map/reduce_scatter | solution.py:88
  344.6 12.9 %collective-permute-start.12 = (bf16[256,1024]{1,0:T(8,128)(2,1)}, bf16[256,1024]{1,0:T(8,128)(2,1)S(1)}, u32[]{:S(2)}, u32[]{:S(2)}) collective-permute-start(bf16[256,1024]{1,0:T(8,128)(2,1)} %get-tuple-element.56), channel_id=1, source_target_pairs={{0,1},{1,0},{2,3},{3,2},{4,5},{5,4},{6,7},{7,6},{8,9},{9,8},{10,11... | collective-permute-start | bytes 1572872 | tf_op jit(solution)/shard_map/ppermute | solution.py:33
  347.2 14.5 %collective-permute-start.14 = (bf16[256,1024]{1,0:T(8,128)(2,1)}, bf16[256,1024]{1,0:T(8,128)(2,1)}, u32[]{:S(2)}, u32[]{:S(2)}) collective-permute-start(bf16[256,1024]{1,0:T(8,128)(2,1)} %fusion.61), channel_id=1, source_target_pairs={{0,2},{1,3},{2,0},{3,1},{4,6},{5,7},{6,4},{7,5},{8,10},{9,11},{10,... | collective-permute-start | bytes 1572872 | tf_op jit(solution)/shard_map/ppermute | solution.py:33
  357.1 7.5 %collective-permute-start.25 = (bf16[256,1024]{1,0:T(8,128)(2,1)}, bf16[256,1024]{1,0:T(8,128)(2,1)}, u32[]{:S(2)}, u32[]{:S(2)}) collective-permute-start(bf16[256,1024]{1,0:T(8,128)(2,1)} %get-tuple-element.53), channel_id=1, source_target_pairs={{0,1},{1,0},{2,3},{3,2},{4,5},{5,4},{6,7},{7,6},{8,9},{9,8},{10,11... | collective-permute-start | bytes 1572872 | tf_op jit(solution)/shard_map/ppermute | solution.py:33
  364.5 7.4 %collective-permute-start.24 = (bf16[256,1024]{1,0:T(8,128)(2,1)}, bf16[256,1024]{1,0:T(8,128)(2,1)S(1)}, u32[]{:S(2)}, u32[]{:S(2)}) collective-permute-start(bf16[256,1024]{1,0:T(8,128)(2,1)} %get-tuple-element.52), channel_id=1, source_target_pairs={{0,1},{1,0},{2,3},{3,2},{4,5},{5,4},{6,7},{7,6},{8,9},{9,8},{10,11... | collective-permute-start | bytes 1572872 | tf_op jit(solution)/shard_map/ppermute | solution.py:33
  366.9 15.7 %collective-permute-start.26 = (bf16[256,1024]{1,0:T(8,128)(2,1)}, bf16[256,1024]{1,0:T(8,128)(2,1)}, u32[]{:S(2)}, u32[]{:S(2)}) collective-permute-start(bf16[256,1024]{1,0:T(8,128)(2,1)} %fusion.57), channel_id=1, source_target_pairs={{0,2},{1,3},{2,0},{3,1},{4,6},{5,7},{6,4},{7,5},{8,10},{9,11},{10,... | collective-permute-start | bytes 1572872 | tf_op jit(solution)/shard_map/ppermute | solution.py:33
  368.9 62.5 %collective-permute-start.30 = (bf16[32,1024]{1,0:T(8,128)(2,1)}, bf16[32,1024]{1,0:T(8,128)(2,1)S(1)}, u32[]{:S(2)}, u32[]{:S(2)}) collective-permute-start(bf16[32,1024]{1,0:T(8,128)(2,1)} %bitcast.299), channel_id=1, source_target_pairs={{0,0},{1,8},{2,16},{3,24},{4,1},{5,9},{6,17},{7,25},{8,2},{9,10},{... | collective-permute-start | bytes 196616 | tf_op jit(solution)/shard_map/ppermute | solution.py:256
  436.8 71.4 %collective-permute-start.27 = (bf16[32,1792]{1,0:T(8,128)(2,1)S(1)}, bf16[32,1792]{1,0:T(8,128)(2,1)S(1)}, u32[]{:S(2)}, u32[]{:S(2)}) collective-permute-start(bf16[32,1792]{1,0:T(8,128)(2,1)S(1)} %get-tuple-element.64), channel_id=1, source_target_pairs={{0,1},{1,0},{2,3},{3,2},{4,5},{5,4},{6,7},{7,6},{8,9},{9,8},{10,11... | collective-permute-start | bytes 344072 | tf_op jit(solution)/shard_map/ppermute | solution.py:33
  507.7 6.0 %collective-permute-start.29 = (bf16[32,1792]{1,0:T(8,128)(2,1)S(1)}, bf16[32,1792]{1,0:T(8,128)(2,1)S(1)}, u32[]{:S(2)}, u32[]{:S(2)}) collective-permute-start(bf16[32,1792]{1,0:T(8,128)(2,1)S(1)} %get-tuple-element.62), channel_id=1, source_target_pairs={{0,3},{1,2},{2,1},{3,0},{4,7},{5,6},{6,5},{7,4},{8,11},{9,10},{10,... | collective-permute-start | bytes 344072 | tf_op jit(solution)/shard_map/ppermute | solution.py:33
  (58 other events, 870.3 us)
Sparse Core Ops, SparseCore 0:
  19.2 46.8 all-gather.8
  68.8 48.5 all-gather.10
  119.5 48.0 all-gather.12
  234.3 63.5 reduce-scatter.8
  301.6 66.2 reduce-scatter.6
  371.6 64.0 reduce-scatter.4
  439.2 66.6 reduce-scatter.10
